TPU v7x, 512 devices: a whole 4x4x16 slice. The times are simulated.
512 devices in a mesh: node: 8 (over y, core), scen: 64 (over z, x).
Axes of the slice: x: 4, y: 4, z: 16, core: 2. Of those that a mesh axis runs over, the one named last changes fastest.
Arguments:
- sample_submatrices: bfloat16 [8192, 128, 1024], P(('node', 'scen')), may hold values from -0.176776695 to 0.176776695
- penalty_weights: float32 [8192, 128], P(('node', 'scen')), may hold values from 0.001 to 10
- sample_patch_pattern: int32 [8192, 8], P(('node', 'scen')), may hold values 0 or 1
- terminal_penalty_entries: float32 [8, 1024], P('node'), may hold values from 0.25 to 4
- terminal_ancestor_coupler: bfloat16 [8, 1024, 256], P('node'), may hold values from -0.1875 to 0.1875
- secondary_penalty_entries: float32 [2, 256], replicated, may hold values from 0.25 to 4
- secondary_base_coupler: bfloat16 [2, 256, 128], replicated, may hold values from -0.375 to 0.375
- opening_penalty_entries: float32 [128], replicated, may hold values from 0.25 to 4
Outputs:
- node_factor: float32 [8, 1024, 1024], P('node', 'scen')
- parent_factor: float32 [2, 256, 256], replicated
- root_factor: float32 [128, 128], replicated
All inputs are finite; a program needn't handle non-finite values. No bound on the sum of `sample_patch_pattern` on one device may be relied on, other than what follows from the above.
Results may differ from a plain program's by a relative error of at most 0.00037.
Values sent between devices are 32-bit elements; how exact they have to be, the bound alone decides.
No kernel may reach another device: no remote copies, remote signals or barrier semaphores. Data moves between devices by JAX's collectives and lax.ppermute only.
A program may use at most 128 MiB of HBM per device.

v0:
```python
import jax
import jax.numpy as jnp
from jax import lax
from jax.sharding import PartitionSpec as P

PARENTS = 2


def column_mask(sample_patch_pattern, width):
    tiles = sample_patch_pattern.shape[1]
    size = width // tiles
    owner = lax.broadcasted_iota(jnp.int32, (tiles, width), 1) // size
    table = (owner == lax.broadcasted_iota(jnp.int32, (tiles, width), 0)).astype(jnp.float32)
    return jnp.dot(sample_patch_pattern.astype(jnp.float32), table, precision=lax.Precision.HIGHEST)


def per_device(
    sample_submatrices,
    penalty_weights,
    sample_patch_pattern,
    terminal_penalty_entries,
    terminal_ancestor_coupler,
    secondary_penalty_entries,
    secondary_base_coupler,
    opening_penalty_entries,
):
    width = sample_submatrices.shape[2]
    patch_field_pattern = column_mask(sample_patch_pattern, width)
    midpoint_extent = (
        sample_submatrices.astype(jnp.float32)
        * jnp.sqrt(penalty_weights)[:, :, None]
        * patch_field_pattern[:, None, :]
    )
    midpoint_extent = midpoint_extent.astype(jnp.bfloat16).reshape(-1, width)
    share_rows = width // lax.axis_size("scen")
    whole_term = lax.dot_general(
        midpoint_extent,
        midpoint_extent,
        (((0,), (0,)), ((), ())),
        preferred_element_type=jnp.float32,
    )
    schur = lax.psum(whole_term, "scen")
    block = schur + jnp.diag(terminal_penalty_entries[0])
    factor = jnp.linalg.cholesky(block)
    first_row = lax.axis_index("scen") * share_rows
    own_rows = lax.dynamic_slice_in_dim(factor, first_row, share_rows, 0)[None]
    reduced = jax.scipy.linalg.solve_triangular(
        factor, terminal_ancestor_coupler[0].astype(jnp.float32), lower=True
    )
    condensed = jnp.dot(reduced.T, reduced, precision=lax.Precision.HIGHEST)
    node_count = lax.axis_size("node")
    parent_ids = jnp.arange(PARENTS, dtype=jnp.int32)
    my_parent = lax.axis_index("node") * PARENTS // node_count
    selector = (parent_ids == my_parent).astype(jnp.float32)
    sums = lax.psum(selector[:, None, None] * condensed[None], "node")
    parent_block = sums + jax.vmap(jnp.diag)(secondary_penalty_entries)
    parent_factor = jnp.linalg.cholesky(parent_block)
    solve_one = lambda fac, rhs: jax.scipy.linalg.solve_triangular(fac, rhs, lower=True)
    parent_reduced = jax.vmap(solve_one)(parent_factor, secondary_base_coupler.astype(jnp.float32))
    pieces = jnp.einsum(
        "bpr,bps->rs", parent_reduced, parent_reduced, precision=lax.Precision.HIGHEST
    )
    root_block = jnp.diag(opening_penalty_entries) + pieces
    root_factor = jnp.linalg.cholesky(root_block)
    return (own_rows, parent_factor, root_factor)


def solution(mesh):
    placed = (
        P(("node", "scen"), None, None),
        P(("node", "scen"), None),
        P(("node", "scen"), None),
        P("node", None),
        P("node", None, None),
        P(),
        P(),
        P(),
    )
    return jax.shard_map(
        per_device,
        mesh=mesh,
        in_specs=placed,
        out_specs=(P("node", "scen", None), P(), P()),
        check_vma=False,
    )
```

profile of v0, /device:TPU:6, one launch (start us, length us, event | category | flops | bytes accessed | tf_op | source)
XLA Modules:
  0.0 879.3 jit_solution(12251882770582183225)
XLA Ops:
  8.9 10.5 %fusion.5 = f32[1024,1024]{0,1:T(8,128)} fusion(bf16[16,128,1024]{2,1,0:T(8,128)(2,1)} %param.8, f32[16,1024]{1,0:T(8,128)S(1)} %convolution_bitcast_fusion, f32[16,128]{1,0:T(8,128)S(1)} %sqrt.3), kind=kOutput, calls=%fused_computation.16 | convolution fusion | flops 4303355904 | bytes 8462336 | tf_op jit(solution)/shard_map/dot_general | solution.py:36
  20.6 292.1 %all-reduce.5.cloned.1.call-done = f32[1024,1024]{0,1:T(8,128)} async-done(((f32[1024,1024]{0,1:T(8,128)}), f32[1024,1024]{0,1:T(8,128)}) %all-reduce.5.cloned.1.call-update) | async-done | bytes 4194320 | tf_op jit(solution)/shard_map/psum | solution.py:42
  312.7 4.8 select_add_fusion
  317.5 5.5 copy.78
  323.0 4.4 fusion.1
  327.5 1.9 copy-done.1
  329.4 11.7 %cholesky.285 = f32[128,128]{1,0:T(8,128)S(1)} custom-call(f32[128,128]{1,0:T(8,128)S(1)} %cholesky.740), custom_call_target="Cholesky" | custom-call | tf_op jit(solution)/shard_map/jit(cholesky)/cholesky | solution.py:44
  341.2 9.8 %custom-call.83 = f32[1,128,128]{1,2,0:T(8,128)S(1)} custom-call(f32[1,128,128]{2,1,0:T(8,128)S(1)} %get-tuple-element.116), custom_call_target="InvertDiagBlocksLowerTriangular" | custom-call | tf_op jit(solution)/shard_map/jit(cholesky)/cholesky | solution.py:44
  354.4 11.7 %cholesky.308 = f32[128,128]{1,0:T(8,128)S(1)} custom-call(f32[128,128]{1,0:T(8,128)S(1)} %cholesky.744), custom_call_target="Cholesky" | custom-call | tf_op jit(solution)/shard_map/jit(cholesky)/cholesky | solution.py:44
  366.4 9.8 %custom-call.84 = f32[1,128,128]{1,2,0:T(8,128)S(1)} custom-call(f32[1,128,128]{2,1,0:T(8,128)S(1)} %get-tuple-element.114), custom_call_target="InvertDiagBlocksLowerTriangular" | custom-call | tf_op jit(solution)/shard_map/jit(cholesky)/cholesky | solution.py:44
  377.4 2.0 copy-done
  379.3 2.4 convolution_subtract_fusion.1
  381.8 11.7 %cholesky.335 = f32[128,128]{1,0:T(8,128)S(1)} custom-call(f32[128,128]{1,0:T(8,128)S(1)} %cholesky.749), custom_call_target="Cholesky" | custom-call | tf_op jit(solution)/shard_map/jit(cholesky)/cholesky | solution.py:44
  394.3 9.8 %custom-call.85 = f32[1,128,128]{1,2,0:T(8,128)S(1)} custom-call(f32[1,128,128]{2,1,0:T(8,128)S(1)} %get-tuple-element.112), custom_call_target="InvertDiagBlocksLowerTriangular" | custom-call | tf_op jit(solution)/shard_map/jit(cholesky)/cholesky | solution.py:44
  405.3 3.5 convolution_subtract_fusion.2
  408.8 11.7 %cholesky.612 = f32[128,128]{1,0:T(8,128)S(1)} custom-call(f32[128,128]{1,0:T(8,128)S(1)} %cholesky.754), custom_call_target="Cholesky" | custom-call | tf_op jit(solution)/shard_map/jit(cholesky)/cholesky | solution.py:44
  421.3 9.8 %custom-call.86 = f32[1,128,128]{1,2,0:T(8,128)S(1)} custom-call(f32[1,128,128]{2,1,0:T(8,128)S(1)} %get-tuple-element.110), custom_call_target="InvertDiagBlocksLowerTriangular" | custom-call | tf_op jit(solution)/shard_map/jit(cholesky)/cholesky | solution.py:44
  432.3 3.2 convolution_subtract_fusion.3
  435.4 11.9 %cholesky.631 = f32[128,128]{1,0:T(8,128)S(1)} custom-call(f32[128,128]{1,0:T(8,128)S(1)} %cholesky.759), custom_call_target="Cholesky" | custom-call | tf_op jit(solution)/shard_map/jit(cholesky)/cholesky | solution.py:44
  448.1 9.8 %custom-call.87 = f32[1,128,128]{1,2,0:T(8,128)S(1)} custom-call(f32[1,128,128]{2,1,0:T(8,128)S(1)} %get-tuple-element.108), custom_call_target="InvertDiagBlocksLowerTriangular" | custom-call | tf_op jit(solution)/shard_map/jit(cholesky)/cholesky | solution.py:44
  459.0 3.2 convolution_subtract_fusion.4
  462.3 11.7 %cholesky.651 = f32[128,128]{1,0:T(8,128)S(1)} custom-call(f32[128,128]{1,0:T(8,128)S(1)} %cholesky.764), custom_call_target="Cholesky" | custom-call | tf_op jit(solution)/shard_map/jit(cholesky)/cholesky | solution.py:44
  474.8 9.8 %custom-call.88 = f32[1,128,128]{1,2,0:T(8,128)S(1)} custom-call(f32[1,128,128]{2,1,0:T(8,128)S(1)} %get-tuple-element.106), custom_call_target="InvertDiagBlocksLowerTriangular" | custom-call | tf_op jit(solution)/shard_map/jit(cholesky)/cholesky | solution.py:44
  485.6 2.9 convolution_subtract_fusion.11
  488.5 11.7 %cholesky.671 = f32[128,128]{1,0:T(8,128)S(1)} custom-call(f32[128,128]{1,0:T(8,128)S(1)} %cholesky.769), custom_call_target="Cholesky" | custom-call | tf_op jit(solution)/shard_map/jit(cholesky)/cholesky | solution.py:44
  501.0 9.8 %custom-call.89 = f32[1,128,128]{1,2,0:T(8,128)S(1)} custom-call(f32[1,128,128]{2,1,0:T(8,128)S(1)} %get-tuple-element.104), custom_call_target="InvertDiagBlocksLowerTriangular" | custom-call | tf_op jit(solution)/shard_map/jit(cholesky)/cholesky | solution.py:44
  511.7 2.2 convolution_subtract_fusion.15
  513.9 11.7 %cholesky.689 = f32[128,128]{1,0:T(8,128)S(1)} custom-call(f32[128,128]{1,0:T(8,128)S(1)} %convolution_subtract_fusion.15), custom_call_target="Cholesky" | custom-call | tf_op jit(solution)/shard_map/jit(cholesky)/cholesky | solution.py:44
  536.8 6.6 fusion.4
  543.4 29.3 %while.2 = (s32[]{:T(128)}, f32[1024,1024]{0,1:T(8,128)}, s32[8,2]{0,1:T(2,128)S(1)}, f32[8,128,128]{2,1,0:T(8,128)}, s32[]{:T(128)}) while((s32[]{:T(128)}, f32[1024,1024]{0,1:T(8,128)}, s32[8,2]{0,1:T(2,128)S(1)}, f32[8,128,128]{2,1,0:T(8,128)}, s32[]{:T(128)}) %tuple.79), condition=%wide.while_cond, body=%wide.while_body.sunk | while | flops 2 | bytes 393329 | solution.py:47
  544.3 2.3 dynamic-slice.15
  548.0 2.3 dynamic-slice.15
  551.6 2.3 dynamic-slice.15
  555.2 2.3 dynamic-slice.15
  558.9 2.3 dynamic-slice.15
  562.5 2.3 dynamic-slice.15
  566.1 2.3 dynamic-slice.15
  569.7 2.2 dynamic-slice.15
  572.7 79.4 %custom-call.90 = f32[8,128,128]{1,2,0:T(8,128)S(1)} custom-call(f32[8,128,128]{2,1,0:T(8,128)} %get-tuple-element.10), custom_call_target="InvertDiagBlocksLowerTriangular" | custom-call | tf_op jit(solution)/shard_map/jit(_solve_triangular)/triangular_solve | solution.py:47
  661.2 1.8 convolution_subtract_fusion.9
  663.3 2.0 convolution_subtract_fusion.14
  670.5 70.3 %all-reduce.7.cloned.1.call-done = f32[2,256,256]{1,2,0:T(8,128)} async-done(((f32[2,256,256]{1,2,0:T(8,128)}), f32[2,256,256]{1,2,0:T(8,128)}) %all-reduce.7.cloned.1.call-update) | async-done | bytes 524304 | tf_op jit(solution)/shard_map/psum | solution.py:55
  743.2 23.6 %custom-call.91 = f32[2,128,128]{2,1,0:T(8,128)S(1)} custom-call(f32[2,128,128]{2,1,0:T(8,128)S(1)} %cholesky.773), custom_call_target="Cholesky" | custom-call | tf_op jit(solution)/shard_map/jit(cholesky)/cholesky | solution.py:57
  767.0 19.7 %custom-call.92 = f32[2,1,128,128]{2,3,1,0:T(8,128)S(1)} custom-call(f32[2,1,128,128]{3,2,1,0:T(8,128)S(1)} %select_bitcast_fusion), custom_call_target="InvertDiagBlocksLowerTriangular" | custom-call | tf_op jit(solution)/shard_map/jit(cholesky)/cholesky | solution.py:57
  787.5 23.5 %custom-call.93 = f32[2,128,128]{2,1,0:T(8,128)S(1)} custom-call(f32[2,128,128]{2,1,0:T(8,128)S(1)} %convolution_subtract_fusion.13), custom_call_target="Cholesky" | custom-call | tf_op jit(solution)/shard_map/jit(cholesky)/cholesky | solution.py:57
  812.6 4.4 while.3
  817.0 39.5 %custom-call.94 = f32[2,2,128,128]{2,3,1,0:T(8,128)S(1)} custom-call(f32[2,2,128,128]{3,2,1,0:T(8,128)S(1)} %bitcast.185), custom_call_target="InvertDiagBlocksLowerTriangular" | custom-call | tf_op jit(solution)/shard_map/vmap(jit(_solve_triangular))/triangular_solve | solution.py:58
  858.5 11.7 %cholesky.729 = f32[128,128]{1,0:T(8,128)S(1)} custom-call(f32[128,128]{1,0:T(8,128)S(1)} %fusion.66), custom_call_target="Cholesky" | custom-call | tf_op jit(solution)/shard_map/jit(cholesky)/cholesky | solution.py:64
  (168 shorter events, 61.0 us)
Async XLA Ops:
  7.2 305.5 %all-reduce.5.cloned.1.call-start = ((), (), s32[]{:S(2)}) async-start(), calls=%async_computation | async-start | bytes 8388608 | tf_op jit(solution)/shard_map/psum | solution.py:42
  19.3 1.0 copy-start.2
  19.3 293.3 %copy-start.4 = (f32[1,1024]{1,0:T(1,128)S(1)}, f32[1,1024]{1,0:T(1,128)}, u32[]{:S(2)}) copy-start(f32[1,1024]{1,0:T(1,128)} %param.11) | copy-start | bytes 12292
  19.4 721.4 %all-reduce.7.cloned.1.call-start = ((), (), s32[]{:S(2)}) async-start(), calls=%async_computation.1 | async-start | bytes 1048576 | tf_op jit(solution)/shard_map/psum | solution.py:55
  327.5 1.9 copy-start.1
  377.4 2.0 copy-start
  663.0 77.8 %copy-start.5 = (f32[2,256]{1,0:T(2,128)S(1)}, f32[2,256]{1,0:T(2,128)}, u32[]{:S(2)}) copy-start(f32[2,256]{1,0:T(2,128)} %param.13) | copy-start | bytes 6148
  787.5 69.1 %copy-start.3 = (bf16[2,256,128]{2,1,0:T(8,128)(2,1)S(1)}, bf16[2,256,128]{2,1,0:T(8,128)(2,1)}, u32[]{:S(2)}) copy-start(bf16[2,256,128]{2,1,0:T(8,128)(2,1)} %param.14) | copy-start | bytes 393220
  811.4 47.0 %copy-start.6 = (f32[128]{0:T(128)S(1)}, f32[128]{0:T(128)}, u32[]{:S(2)}) copy-start(f32[128]{0:T(128)} %param.15) | copy-start | bytes 1540
Sparse Core Ops, SparseCore 0:
  19.5 293.1 all-reduce.4
  668.5 72.2 all-reduce.6
where the time goes:
time: 886 us; the launch traced here: 879 us
  other arithmetic  387 us (44%)
  waiting for transfers between devices  362 us (41%)
  matrix products  55.4 us (6%)
  local copies, waits for them, and re-layouts  53.4 us (6%)
  between operations  20.3 us (2%)
    psum x1, waiting for transfers between devices, per_device(): schur = lax.psum(whole_term, 'scen')  292 us
    another operation x33, other arithmetic, per_device(): factor = jnp.linalg.cholesky(block)  168 us
    another operation x3, other arithmetic, per_device(): jax.scipy.linalg.solve_triangular(factor, terminal_ancestor_coupler[0].as...  86 us
    psum x1, waiting for transfers between devices, per_device(): sums = lax.psum(selector[:, None, None] * condensed[None], 'node')  70.3 us
    another operation x8, other arithmetic, per_device(): parent_factor = jnp.linalg.cholesky(parent_block)  67.1 us
    another operation x3, other arithmetic, per_device(): jax.scipy.linalg.solve_triangular(fac, rhs, lower=True)  39.7 us
    another operation x50, local copies, waits for them, and re-layouts  33.2 us
    another operation x14, matrix products, per_device(): factor = jnp.linalg.cholesky(block)  26.4 us
  transfers between devices with their start and end apart: 2, of which 2 were waited for; matrix products, arithmetic and copies ran while one was open for 0% of the time, Pallas kernels for 0%

commit v1 on v0

v1 whole, which is shorter than its diff:
```python
import jax
import jax.numpy as jnp
from jax import lax
from jax.experimental import pallas as pl
from jax.experimental.pallas import tpu as pltpu
from jax.sharding import Mesh, PartitionSpec as P

F = jnp.float32
HI = lax.Precision.HIGHEST

NEWT=1
def recip(d):
    r=pl.reciprocal(d,approx=True)
    for _ in range(NEWT): r=r*(2.0-d*r)
    return r
def chol_tiles(chains):
    row=lax.broadcasted_iota(jnp.int32,(8,128),0); col=lax.broadcasted_iota(jnp.int32,(8,128),1)
    full=lambda v: jnp.broadcast_to(v,(8,128))
    T=len(chains[0])
    st=[]
    for tiles in chains:
        st.append((list(tiles),[(col==row+8*t).astype(F) for t in range(T)],[],[]))
    for g in range(T):
        for Xa,Xw,U,W in st:
            b0=8*g
            C={t:[full(Xa[t][:,b0+k:b0+k+1]) for k in range(8)] for t in range(g,T)}
            s=[[full(C[g][k][i:i+1,:]) if i>=k else None for k in range(8)] for i in range(8)]
            Ra=[full(Xa[g][i:i+1,:]) for i in range(8)]
            Rw=[full(Xw[g][i:i+1,:]) for i in range(8)]
            upd=[]
            u=w=jnp.zeros((8,128),F)
            for k in range(0,8,2):
                k1=k+1
                a=s[k][k]; b=s[k1][k]; c=s[k1][k1]
                det=a*c-b*b
                rd=recip(det); ra=recip(a)
                ia=c*rd; ib=b*rd; ic=a*rd
                for l in range(k+2,8):
                    p=(c*s[l][k]-b*s[l][k1])*rd; q=(a*s[l][k1]-b*s[l][k])*rd
                    for i in range(l,8): s[i][l]=s[i][l]-(p*s[i][k]+q*s[i][k1])
                    Ra[l]=Ra[l]-(p*Ra[k]+q*Ra[k1]); Rw[l]=Rw[l]-(p*Rw[k]+q*Rw[k1])
                    for t in range(g+1,T): C[t][l]=C[t][l]-(p*C[t][k]+q*C[t][k1])
                upd.append((ia,ib,ic))
                m=b*ra
                q0=lax.rsqrt(a); q1=lax.rsqrt(det*ra)
                u=jnp.where(row==k,Ra[k]*q0,jnp.where(row==k1,(Ra[k1]-m*Ra[k])*q1,u))
                w=jnp.where(row==k,Rw[k]*q0,jnp.where(row==k1,(Rw[k1]-m*Rw[k])*q1,w))
            for t in range(g+1,T):
                for k in range(0,8,2):
                    ia,ib,ic=upd[k//2]
                    x=C[t][k]; y=C[t][k+1]
                    c0=ia*x-ib*y; c1=ic*y-ib*x
                    Xa[t]=Xa[t]-(c0*Ra[k]+c1*Ra[k+1]); Xw[t]=Xw[t]-(c0*Rw[k]+c1*Rw[k+1])
            U.append(jnp.where(col>=row+b0,u,0.0)); W.append(w)
    return [(U,W) for _,_,U,W in st]
OFF=[sum(8-q for q in range(k)) for k in range(9)]
NC=4
def schur_kernel(x_hbm, w_ref, p_ref, s_ref, x_v, half, ht, sq, sem):
    n=x_v.shape[0]; c=n//NC
    cps=[pltpu.make_async_copy(x_hbm.at[pl.ds(q*c,c)],x_v.at[pl.ds(q*c,c)],sem.at[q]) for q in range(NC)]
    for cp in cps: cp.start()
    rw=jnp.sqrt(w_ref[...])
    sq[...]=jnp.concatenate([rw]*8,0).T
    for q in range(NC):
        cps[q].wait()
        for s in range(q*c,(q+1)*c):
            col=jnp.broadcast_to(sq[:,s:s+1],(128,128))
            for j in range(8):
                m=p_ref[s,j].astype(F)
                half[s*128:(s+1)*128,j*128:(j+1)*128]=(x_v[s,:,j*128:(j+1)*128].astype(F)*col*m).astype(jnp.bfloat16)
            for j in range(4):
                ht[j*256:(j+1)*256,s*128:(s+1)*128]=half[s*128:(s+1)*128,j*256:(j+1)*256].T
    for J in range(4):
        for I in range(J,4):
            r=jnp.dot(ht[I*256:(I+1)*256,:],half[:,J*256:(J+1)*256],preferred_element_type=F)
            for a in range(2):
                for b in range(2):
                    i,j=2*I+a,2*J+b
                    if i>=j:
                        o=(OFF[j]+i-j)*128
                        s_ref[o:o+128,:]=r[a*128:(a+1)*128,b*128:(b+1)*128]
def schur(x,w,p):
    n=x.shape[0]
    return pl.pallas_call(schur_kernel,out_shape=jax.ShapeDtypeStruct((36*128,128),F),
      in_specs=[pl.BlockSpec(memory_space=pl.ANY),pl.BlockSpec(memory_space=pltpu.VMEM),pl.BlockSpec(memory_space=pltpu.SMEM)],
      out_specs=pl.BlockSpec(memory_space=pltpu.VMEM),
      scratch_shapes=[pltpu.VMEM((n,128,1024),jnp.bfloat16),pltpu.VMEM((n*128,1024),jnp.bfloat16),pltpu.VMEM((1024,n*128),jnp.bfloat16),pltpu.VMEM((128,128),F),pltpu.SemaphoreType.DMA((NC,))],
      compiler_params=pltpu.CompilerParams(vmem_limit_bytes=40<<20),
      cost_estimate=pl.CostEstimate(flops=1<<32,bytes_accessed=6<<20,transcendentals=2048),
      name="schur_term")(x,w,p)
def dnt(a,b,prec=HI):
    return lax.dot_general(a,b,(((1,),(1,)),((),())),precision=prec,preferred_element_type=F)
NB=8; B=128
OFF=[sum(NB-q for q in range(k)) for k in range(NB+1)]
def chol_vals(ds):
    res=chol_tiles([[d[8*t:8*t+8,:] for t in range(16)] for d in ds])
    return [(jnp.concatenate(U,0).T, jnp.concatenate(W,0)) for U,W in res]
def diag_mat(v):
    r=lax.broadcasted_iota(jnp.int32,(128,128),0); c=lax.broadcasted_iota(jnp.int32,(128,128),1)
    return jnp.where(r==c,jnp.broadcast_to(v,(128,128)),0.0)
def node_kernel(row0_ref, s_ref, diag_ref, ct_ref, own_ref, cond_ref, *panels):
    for k in range(NB):
        n=(NB-k)*B
        panels[k][0:n,:]=s_ref[OFF[k]*B:OFF[k+1]*B,:]
        panels[k][0:B,:]=panels[k][0:B,:]+diag_mat(diag_ref[:,k*B:(k+1)*B])
        panels[k][n:n+256,:]=ct_ref[:,k*B:(k+1)*B]
    for k in range(NB):
        (L,W),=chol_vals([panels[k][0:B,:]])
        n=(NB-k)*B+256
        lp=dnt(panels[k][B:n,:],W)
        panels[k][0:B,:]=L
        panels[k][B:n,:]=lp
        for j in range(k+1,NB):
            o=(j-k)*B
            panels[j][...]=panels[j][...]-dnt(panels[k][o:n,:],panels[k][o:o+B,:])
    acc=None
    for k in range(NB):
        n=(NB-k)*B
        c=panels[k][n:n+256,:]
        t=dnt(c,c)
        acc=t if acc is None else acc+t
    cond_ref[...]=acc
    r0=row0_ref[0]
    b=r0//B; off=r0-b*B
    own_ref[...]=jnp.zeros(own_ref.shape,F)
    for k in range(NB):
        @pl.when(b>=k)
        def _():
            own_ref[:,k*B:(k+1)*B]=panels[k][pl.ds(pl.multiple_of((b-k)*B+off,16),16),:]
def node_factor(row0, s, diag, ct):
    return pl.pallas_call(node_kernel,
      out_shape=[jax.ShapeDtypeStruct((16,1024),F),jax.ShapeDtypeStruct((256,256),F)],
      in_specs=[pl.BlockSpec(memory_space=pltpu.SMEM)]+[pl.BlockSpec(memory_space=pltpu.VMEM)]*3,
      out_specs=[pl.BlockSpec(memory_space=pltpu.VMEM)]*2,
      scratch_shapes=[pltpu.VMEM(((10-k)*B,B),F) for k in range(NB)],
      compiler_params=pltpu.CompilerParams(vmem_limit_bytes=40<<20),
      cost_estimate=pl.CostEstimate(flops=1<<32,bytes_accessed=8<<20,transcendentals=1<<14),
      name="node_factor")(row0,s,diag,ct)
def tail_kernel(s_ref, diag_ref, bt_ref, od_ref, pf_ref, rf_ref):
    d0=[s_ref[p,0:B,:]+diag_mat(diag_ref[p:p+1,0:B]) for p in range(2)]
    r0=chol_vals(d0)
    d1=[];lb0=[];l10=[]
    for p in range(2):
        L,W=r0[p]
        l10.append(dnt(s_ref[p,B:2*B,:],W)); lb0.append(dnt(bt_ref[p,:,0:B],W))
        d1.append(s_ref[p,2*B:,:]+diag_mat(diag_ref[p:p+1,B:])-dnt(l10[p],l10[p]))
        pf_ref[p,0:B,0:B]=L; pf_ref[p,0:B,B:]=jnp.zeros((B,B),F); pf_ref[p,B:,0:B]=l10[p]
    r1=chol_vals(d1)
    root=diag_mat(od_ref[...])
    for p in range(2):
        L,W=r1[p]
        pf_ref[p,B:,B:]=L
        lb1=dnt(bt_ref[p,:,B:]-dnt(lb0[p],l10[p]),W)
        root=root+dnt(lb0[p],lb0[p])+dnt(lb1,lb1)
    (L,_),=chol_vals([root])
    rf_ref[...]=L
def tail(s,diag,bt,od):
    return pl.pallas_call(tail_kernel,
      out_shape=[jax.ShapeDtypeStruct((2,256,256),F),jax.ShapeDtypeStruct((128,128),F)],
      in_specs=[pl.BlockSpec(memory_space=pltpu.VMEM)]*4,
      out_specs=[pl.BlockSpec(memory_space=pltpu.VMEM)]*2,
      compiler_params=pltpu.CompilerParams(vmem_limit_bytes=40<<20),
      name="tail")(s,diag,bt,od)
def per_device(samples, weights, pattern, diag, coupler, diag2, coupler2, diag3):
    s = schur(samples, weights, pattern)
    s = lax.all_to_all(s, "x", 0, 0, tiled=True).reshape(4, 1152, 128).sum(0)
    s = lax.all_to_all(s, "z", 0, 0, tiled=True).reshape(16, 72, 128).sum(0)
    s = jnp.broadcast_to(s[None], (16, 72, 128)).reshape(1152, 128)
    s = lax.all_to_all(s, "z", 0, 0, tiled=True)
    s = jnp.broadcast_to(s[None], (4, 1152, 128)).reshape(4608, 128)
    s = lax.all_to_all(s, "x", 0, 0, tiled=True)
    row0 = (lax.axis_index("z") * 4 + lax.axis_index("x")) * 16
    own, cond = node_factor(row0.reshape(1).astype(jnp.int32), s, diag, coupler[0].astype(F).T)
    low = jnp.concatenate([cond[:128, :128], cond[128:, :128], cond[128:, 128:]], 0)
    low = low + lax.ppermute(low, "core", [(0, 1), (1, 0)])
    low = lax.all_gather(low, "y", axis=0)
    low = low.reshape(2, 2, 384, 128).sum(1)
    parent, root = tail(low, diag2, jnp.swapaxes(coupler2.astype(F), 1, 2), diag3[None])
    return own[None], parent, root


def solution(mesh):
    sizes = mesh.devices.shape
    devices = mesh.devices.reshape(4, 2, 16, 4)
    split = Mesh(devices, ("y", "core", "z", "x"))
    node, scen = ("y", "core"), ("z", "x")
    return jax.shard_map(
        per_device,
        mesh=split,
        in_specs=(P(node + scen, None, None), P(node + scen, None), P(node + scen, None), P(node, None), P(node, None, None), P(), P(), P()),
        out_specs=(P(node, scen, None), P(), P()),
        check_vma=False,
    )
```

time: 886 us -> 259 us (0.29)
  the two profiles are of different devices: /device:TPU:6 before, /device:TPU:40 now
where the time goes in v1:
time: 259 us; the launch traced here: 254 us
  blocking collectives  134 us (52%)
  Pallas kernels  78.6 us (30%)
  waiting for transfers between devices  26.1 us (10%)
  local copies, waits for them, and re-layouts  6.41 us (2%)
  starting transfers between devices  6.15 us (2%)
    pallas_call x1, Pallas kernels, node_factor(): pl.pallas_call(node_kernel, out_shape=[jax.ShapeDtypeStruct((16, 1024), F...  50.3 us
    all_to_all x1, blocking collectives, per_device(): s = lax.all_to_all(s, 'z', 0, 0, tiled=True).reshape(16, 72, 128).sum(0)  48.3 us
    all_to_all x1, blocking collectives, per_device(): s = lax.all_to_all(s, 'z', 0, 0, tiled=True)  37.7 us
    all_to_all x1, blocking collectives, per_device(): s = lax.all_to_all(s, 'x', 0, 0, tiled=True).reshape(4, 1152, 128).sum(0)  33.2 us
    all_to_all x1, waiting for transfers between devices, per_device(): s = lax.all_to_all(s, 'x', 0, 0, tiled=True)  24.7 us
    pallas_call x1, Pallas kernels, tail(): pl.pallas_call(tail_kernel, out_shape=[jax.ShapeDtypeStruct((2, 256, 256)...  21.7 us
    all_gather x1, blocking collectives, per_device(): low = lax.all_gather(low, 'y', axis=0)  14.7 us
    pallas_call x1, Pallas kernels, schur(): pl.pallas_call(schur_kernel, out_shape=jax.ShapeDtypeStruct((36 * 128, 12...  6.55 us
  transfers between devices with their start and end apart: 2, of which 2 were waited for; matrix products, arithmetic and copies ran while one was open for 1% of the time, Pallas kernels for 0%

profile of v1, /device:TPU:40, one launch (start us, length us, event | category | flops | bytes accessed | tf_op | source)
XLA Modules:
  0.0 253.6 jit_solution(10741853908678288930)
XLA Ops:
  0.6 0.8 copy.14.p_ref
  1.4 0.0 copy-start.2
  1.4 2.2 copy-done.2
  3.6 0.0 copy-start.3
  3.6 0.7 copy-done.3
  4.3 6.5 %schur_term.1 = f32[4608,128]{1,0:T(8,128)S(1)} custom-call(bf16[16,128,1024]{2,1,0:T(8,128)(2,1)S(1)} %copy-done.2, f32[16,128]{1,0:T(8,128)S(1)} %copy-done.3, s32[16,8]{1,0:T(8,128)S(1)} %copy.14.p_ref), custom_call_target="tpu_custom_call" | custom-call | flops 4294967296 | bytes 6291456 | tf_op jit(solution)/shard_map/schur_term/pallas_call | solution.py:84
  10.8 33.2 %all_to_all.32 = f32[4,1152,128]{2,1,0:T(8,128)S(1)} all-to-all(f32[4,1152,128]{2,1,0:T(8,128)S(1)} %bitcast.16), channel_id=1, replica_groups=mesh['y'=4,'core'=2,'z'=16,'x'=4] {'x'}, dimensions={0} | all-to-all | bytes 4718592 | tf_op jit(solution)/shard_map/all_to_all | solution.py:166
  44.1 0.2 reduce_sum.27
  44.2 48.3 %all_to_all.33 = f32[16,72,128]{2,1,0:T(8,128)S(1)} all-to-all(f32[16,72,128]{2,1,0:T(8,128)S(1)} %bitcast.19), channel_id=1, replica_groups=mesh['y'=4,'core'=2,'z'=16,'x'=4] {'z'}, dimensions={0} | all-to-all | bytes 1179648 | tf_op jit(solution)/shard_map/all_to_all | solution.py:167
  92.6 37.7 %all_to_all.34 = f32[16,72,128]{2,1,0:T(8,128)S(1)} all-to-all(f32[16,72,128]{2,1,0:T(8,128)S(1)} %broadcast_in_dim.20), channel_id=1, replica_groups=mesh['y'=4,'core'=2,'z'=16,'x'=4] {'z'}, dimensions={0} | all-to-all | bytes 1179648 | tf_op jit(solution)/shard_map/all_to_all | solution.py:169
  130.4 1.6 broadcast_in_dim.22
  131.9 0.0 copy-start.5
  131.9 0.0 copy-start.6
  131.9 4.2 %all-to-all-start.3 = ((f32[4,1152,128]{2,1,0:T(8,128)}), f32[4,1152,128]{2,1,0:T(8,128)S(1)}, u32[]{:S(2)}, u32[]{:S(2)}) async-start(f32[4,1152,128]{2,1,0:T(8,128)} %broadcast_in_dim.22), calls=%async_computation.3 | async-start | bytes 4718592 | tf_op jit(solution)/shard_map/all_to_all | solution.py:171
  136.2 0.0 copy-start.4
  136.2 0.0 copy-done.5
  136.2 1.0 copy.15
  137.2 0.0 copy-done.6
  137.2 0.1 copy.16
  137.3 1.1 convert_bitcast_fusion.ct_ref
  138.5 24.7 %all-to-all-done.3 = f32[4,1152,128]{2,1,0:T(8,128)S(1)} async-done(((f32[4,1152,128]{2,1,0:T(8,128)}), f32[4,1152,128]{2,1,0:T(8,128)S(1)}, u32[]{:S(2)}, u32[]{:S(2)}) %all-to-all-start.3) | async-done | bytes 2359328 | tf_op jit(solution)/shard_map/all_to_all | solution.py:171
  163.2 0.0 copy-done.4
  163.2 50.3 %node_factor.1 = (f32[16,1024]{1,0:T(8,128)}, f32[256,256]{1,0:T(8,128)S(1)}) custom-call(s32[1]{0:T(128)} %bitcast.row0_ref, f32[4608,128]{1,0:T(8,128)S(1)} %bitcast.15, f32[1,1024]{1,0:T(1,128)S(1)} %copy-done.4, f32[256,1024]{1,0:T(8,128)S(1)} %convert_bitcast_fusion.ct_ref), custom_call_target="tpu_custom_call" | custom-call | flops 4294967296 | bytes 8388608 | tf_op jit(solution)/shard_map/node_factor/pallas_call | solution.py:131
  213.6 0.0 copy-start
  213.6 0.0 copy-start.1
  213.6 1.9 collective-permute-start
  215.6 1.4 collective-permute-done
  217.0 14.7 %all-gather = f32[1536,128]{1,0:T(8,128)S(1)} all-gather(f32[384,128]{1,0:T(8,128)S(1)} %fusion), channel_id=2, replica_groups=mesh['y'=4,'core'=2,'z'=16,'x'=4] {'y'}, dimensions={0}, use_global_device_ids=true | all-gather | bytes 983040 | tf_op jit(solution)/shard_map/all_gather | solution.py:176
  231.7 0.1 reduce_sum.29.s_ref
  231.7 0.0 copy-done
  231.7 0.0 copy-done.1
  231.7 21.7 %tail.1 = (f32[2,256,256]{2,1,0:T(8,128)}, f32[128,128]{1,0:T(8,128)}) custom-call(f32[2,384,128]{2,1,0:T(8,128)S(1)} %reduce_sum.29.s_ref, f32[2,256]{1,0:T(2,128)S(1)} %copy-done, f32[2,128,256]{2,1,0:T(8,128)S(1)} %convert_bitcast_fusion.1.bt_ref, f32[1,128]{1,0:T(1,128)S(1)} %bitcast.17), custom_call_target="tpu_custom_call" | custom-call | tf_op jit(solution)/shard_map/tail/pallas_call | solution.py:158
  (7 shorter events, 0.2 us)
Async XLA Ops:
  1.4 2.2 copy-start.2
  3.6 0.7 copy-start.3
  131.9 4.3 %copy-start.5 = (bf16[1,1024,256]{2,1,0:T(8,128)(2,1)S(1)}, bf16[1,1024,256]{2,1,0:T(8,128)(2,1)}, u32[]{:S(2)}) copy-start(bf16[1,1024,256]{2,1,0:T(8,128)(2,1)} %param.12) | copy-start | bytes 1572868
  131.9 5.3 %copy-start.6 = (bf16[2,256,128]{2,1,0:T(8,128)(2,1)S(1)}, bf16[2,256,128]{2,1,0:T(8,128)(2,1)}, u32[]{:S(2)}) copy-start(bf16[2,256,128]{2,1,0:T(8,128)(2,1)} %param.14) | copy-start | bytes 393220
  131.9 31.3 %all-to-all-start.3 = ((f32[4,1152,128]{2,1,0:T(8,128)}), f32[4,1152,128]{2,1,0:T(8,128)S(1)}, u32[]{:S(2)}, u32[]{:S(2)}) async-start(f32[4,1152,128]{2,1,0:T(8,128)} %broadcast_in_dim.22), calls=%async_computation.3 | async-start | bytes 4718592 | tf_op jit(solution)/shard_map/all_to_all | solution.py:171
  136.2 27.0 %copy-start.4 = (f32[1,1024]{1,0:T(1,128)S(1)}, f32[1,1024]{1,0:T(1,128)}, u32[]{:S(2)}) copy-start(f32[1,1024]{1,0:T(1,128)} %diag_ref.2) | copy-start | bytes 12292
  213.6 18.2 %copy-start = (f32[2,256]{1,0:T(2,128)S(1)}, f32[2,256]{1,0:T(2,128)}, u32[]{:S(2)}) copy-start(f32[2,256]{1,0:T(2,128)} %diag_ref.3) | copy-start | bytes 6148
  213.6 18.2 %copy-start.1 = (f32[128]{0:T(128)S(1)}, f32[128]{0:T(128)}, u32[]{:S(2)}) copy-start(f32[128]{0:T(128)} %param.15) | copy-start | bytes 1540
  213.6 3.3 %collective-permute-start = (f32[384,128]{1,0:T(8,128)S(1)}, f32[384,128]{1,0:T(8,128)S(1)}, u32[]{:S(2)}, u32[]{:S(2)}) collective-permute-start(f32[384,128]{1,0:T(8,128)S(1)} %pad_maximum_fusion), channel_id=1, source_target_pairs={{0,64},{64,0},{1,65},{65,1},{2,66},{66,2},{3,67},{67,3},{4,68},{68... | collective-permute-start | bytes 589832 | tf_op jit(solution)/shard_map/ppermute | solution.py:175
